TPU v7x, 256 devices: a whole 4x4x8 slice. The times are simulated.
256 devices in a mesh: roll: 32 (over z, y_lo, core), kv: 8 (over y_hi, x).
Axes of the slice: x: 4, y: 4 (y_hi: 2, y_lo: 2; y = y_hi * 2 + y_lo), z: 8, core: 2. Of those that a mesh axis runs over, the one named last changes fastest.
Arguments:
- prompt_q: bfloat16 [2048, 8192], P('roll', 'kv'), may hold values from -144 to 144
- prompt_k: bfloat16 [2048, 1024], P('roll', 'kv'), may hold values from -6 to 6
- prompt_v: bfloat16 [2048, 1024], P('roll', 'kv'), may hold values from -6 to 6
- prompt_do: bfloat16 [2048, 8192], P('roll', 'kv'), may hold values from -6 to 6
- suffix_q: bfloat16 [32, 256, 8192], P('roll', None, 'kv'), may hold values from -144 to 144
- suffix_k: bfloat16 [32, 256, 1024], P('roll', None, 'kv'), may hold values from -6 to 6
- suffix_v: bfloat16 [32, 256, 1024], P('roll', None, 'kv'), may hold values from -6 to 6
- suffix_do: bfloat16 [32, 256, 8192], P('roll', None, 'kv'), may hold values from -6 to 6
- lengths: int32 [32], P('roll'), may hold values from 128 to 256, as said below
- key_weight: bfloat16 [8192, 1024], P(None, 'kv'), may hold values from -0.1875 to 0.1875
- value_weight: bfloat16 [8192, 1024], P(None, 'kv'), may hold values from -0.1875 to 0.1875
Outputs:
- prompt_dq: bfloat16 [2048, 8192], P('roll', 'kv')
- prompt_dk: bfloat16 [2048, 1024], P('roll', 'kv')
- prompt_dv: bfloat16 [2048, 1024], P('roll', 'kv')
- suffix_dq: bfloat16 [32, 256, 8192], P('roll', None, 'kv')
- suffix_dk: bfloat16 [32, 256, 1024], P('roll', None, 'kv')
- suffix_dv: bfloat16 [32, 256, 1024], P('roll', None, 'kv')
- input_grad: bfloat16 [2048, 8192], P(('roll', 'kv'))
Inputs may be any that keep to these rules, and one draw needn't show every extreme that they name: `lengths`: multiples of 128; some rollout has 256.
All inputs are finite; a program needn't handle non-finite values.
Results may differ from a plain program's by a relative error of at most 0.0057.
Values may be sent and summed in bfloat16 or wider, within the bound.
A program may use at most 64 MiB of HBM per device.

v0:
```python
import jax
import jax.numpy as jnp
from jax import lax
from jax.sharding import PartitionSpec as P

HD = 128


neg_big = -1e30


def block_size(count, limit):
    size = max(1, min(count, limit))
    while count % size:
        size -= 1
    return size


def stats_block(carry, queries, kblk, allowed, scale):
    score = jnp.einsum("rkgd,nkd->kgrn", queries, kblk, preferred_element_type=jnp.float32) * scale
    high, total = carry
    top = jnp.max(jnp.where(allowed, score, neg_big), axis=-1)
    new_high = jnp.maximum(high, top)
    expo = jnp.where(allowed, jnp.exp(score - new_high[..., None]), 0.0)
    factor = jnp.exp(high - new_high)
    return (new_high, total * factor + jnp.sum(expo, axis=-1))


def delta_block(queries, grads_out, kblk, vblk, allowed, logsum, scale):
    score = jnp.einsum("rkgd,nkd->kgrn", queries, kblk, preferred_element_type=jnp.float32) * scale
    dprob = jnp.einsum("rkgd,nkd->kgrn", grads_out, vblk, preferred_element_type=jnp.float32)
    prob = jnp.where(allowed, jnp.exp(score - logsum[..., None]), 0.0)
    return jnp.sum(prob * dprob, axis=-1)


def probs_block(queries, grads_out, kblk, vblk, allowed, logsum, delta, scale):
    score = jnp.einsum("rkgd,nkd->kgrn", queries, kblk, preferred_element_type=jnp.float32) * scale
    dprob = jnp.einsum("rkgd,nkd->kgrn", grads_out, vblk, preferred_element_type=jnp.float32)
    prob = jnp.where(allowed, jnp.exp(score - logsum[..., None]), 0.0)
    dscore = (prob * (dprob - delta[..., None])).astype(jnp.bfloat16)
    probh = prob.astype(jnp.bfloat16)
    return (dscore, probh)


def grads_block(queries, grads_out, kblk, vblk, allowed, logsum, delta, scale):
    dscore, probh = probs_block(queries, grads_out, kblk, vblk, allowed, logsum, delta, scale)
    dquery = jnp.einsum("kgrn,nkd->rkgd", dscore, kblk, preferred_element_type=jnp.float32)
    return (dscore, probh, dquery)


def combine_stats(first, second):
    high = jnp.maximum(first[0], second[0])
    fa = jnp.exp(first[0] - high)
    fb = jnp.exp(second[0] - high)
    return (high, first[1] * fa + second[1] * fb)


def stats_piece(carry, piece, start, queries, qpos, scale):
    keys, values = piece
    count = keys.shape[0]
    heads = queries.shape[1]
    width = queries.shape[3]
    size = block_size(count, 512 // heads)

    def stats_step(index, state):
        first = index * size
        kblk = lax.dynamic_slice_in_dim(keys, first, size, 0).reshape(size, heads, width)
        kpos = start + first + lax.iota(jnp.int32, size)
        allowed = (kpos[None, :] <= qpos[:, None])[None, None]
        return stats_block(state, queries, kblk, allowed, scale)

    return lax.fori_loop(0, count // size, stats_step, carry)


def delta_piece(carry, keys, values, queries, grads_out, qpos, logsum, scale):
    count = keys.shape[0]
    heads = queries.shape[1]
    width = queries.shape[3]
    size = block_size(count, 512 // heads)

    def delta_step(index, state):
        first = index * size
        kblk = lax.dynamic_slice_in_dim(keys, first, size, 0).reshape(size, heads, width)
        vblk = lax.dynamic_slice_in_dim(values, first, size, 0).reshape(size, heads, width)
        kpos = first + lax.iota(jnp.int32, size)
        allowed = (kpos[None, :] <= qpos[:, None])[None, None]
        return state + delta_block(queries, grads_out, kblk, vblk, allowed, logsum, scale)

    return lax.fori_loop(0, count // size, delta_step, carry)


def grads_piece(carry, piece, start, queries, grads_out, qpos, logsum, delta, scale, prompt_rows):
    keys, values = piece
    count = keys.shape[0]
    heads = queries.shape[1]
    width = queries.shape[3]
    size = block_size(count, 512 // heads)

    def grads_step(index, state):
        dquery, dk_suffix, dv_suffix, dk_prompt, dv_prompt = state
        first = index * size
        kblk = lax.dynamic_slice_in_dim(keys, first, size, 0).reshape(size, heads, width)
        vblk = lax.dynamic_slice_in_dim(values, first, size, 0).reshape(size, heads, width)
        kpos = start + first + lax.iota(jnp.int32, size)
        allowed = (kpos[None, :] <= qpos[:, None])[None, None]
        dscore, probh, dq_part = grads_block(
            queries, grads_out, kblk, vblk, allowed, logsum, delta, scale
        )
        spot = start + first
        dk_s = jnp.einsum(
            "kgrn,rkgd->nkd",
            dscore[:, :, prompt_rows:],
            queries[prompt_rows:],
            preferred_element_type=jnp.float32,
        )
        dv_s = jnp.einsum(
            "kgrn,rkgd->nkd",
            probh[:, :, prompt_rows:],
            grads_out[prompt_rows:],
            preferred_element_type=jnp.float32,
        )
        dk_p = jnp.einsum(
            "kgrn,rkgd->nkd",
            dscore[:, :, :prompt_rows],
            queries[:prompt_rows],
            preferred_element_type=jnp.float32,
        )
        dv_p = jnp.einsum(
            "kgrn,rkgd->nkd",
            probh[:, :, :prompt_rows],
            grads_out[:prompt_rows],
            preferred_element_type=jnp.float32,
        )
        dk_suffix = lax.dynamic_update_slice_in_dim(
            dk_suffix, dk_s.reshape(size, heads * width), spot, 0
        )
        dv_suffix = lax.dynamic_update_slice_in_dim(
            dv_suffix, dv_s.reshape(size, heads * width), spot, 0
        )
        dk_prompt = lax.dynamic_update_slice_in_dim(
            dk_prompt, dk_p.reshape(size, heads * width), spot, 0
        )
        dv_prompt = lax.dynamic_update_slice_in_dim(
            dv_prompt, dv_p.reshape(size, heads * width), spot, 0
        )
        return (dquery + dq_part, dk_suffix, dv_suffix, dk_prompt, dv_prompt)

    return lax.fori_loop(0, count // size, grads_step, carry)


def body(
    prompt_q,
    prompt_k,
    prompt_v,
    prompt_do,
    suffix_q,
    suffix_k,
    suffix_v,
    suffix_do,
    lengths,
    key_weight,
    value_weight,
):
    block = prompt_k.shape[0]
    kl_width = prompt_k.shape[1]
    width = HD
    heads = kl_width // width
    group = prompt_q.shape[1] // kl_width
    rolls = suffix_q.shape[0]
    span = suffix_q.shape[1]
    total = block * lax.axis_size("roll")
    scale = width ** (-0.5)
    rows = block + rolls * span
    position = lax.iota(jnp.int32, span)
    live = position[None, :] < lengths[:, None]
    masked_do = jnp.where(live[:, :, None], suffix_do, jnp.zeros_like(suffix_do))
    queries = jnp.concatenate([prompt_q, suffix_q.reshape(rolls * span, -1)], axis=0).reshape(
        rows, heads, group, width
    )
    grads_out = jnp.concatenate([prompt_do, masked_do.reshape(rolls * span, -1)], axis=0).reshape(
        rows, heads, group, width
    )
    qpos = jnp.concatenate(
        [
            lax.axis_index("roll") * block + lax.iota(jnp.int32, block),
            jnp.full((rolls * span,), total, jnp.int32),
        ]
    )
    start_stats = (
        jnp.full((heads, group, rows), neg_big, jnp.float32),
        jnp.zeros((heads, group, rows), jnp.float32),
    )
    whole = (
        lax.all_gather(prompt_k, "roll", axis=0, tiled=True),
        lax.all_gather(prompt_v, "roll", axis=0, tiled=True),
    )
    all_keys, all_values = whole
    prompt_stats = stats_piece(start_stats, whole, 0, queries, qpos, scale)
    own_q = suffix_q.reshape(rolls, span, heads, group, width)
    own_do = masked_do.reshape(rolls, span, heads, group, width)
    own_k = suffix_k.reshape(rolls, span, heads, width)
    own_v = suffix_v.reshape(rolls, span, heads, width)
    self_ok = (position[None, None, :] <= position[None, :, None]) & (
        position[None, None, :] < lengths[:, None, None]
    )
    self_start = (
        jnp.full((heads, group, span), neg_big, jnp.float32),
        jnp.zeros((heads, group, span), jnp.float32),
    )

    def self_stats(q_one, k_one, ok_one):
        return stats_block(self_start, q_one, k_one, ok_one[None, None], scale)

    own_stats = jax.vmap(self_stats)(own_q, own_k, self_ok)
    pad_rows = (
        jnp.full((heads, group, block), neg_big, jnp.float32),
        jnp.zeros((heads, group, block), jnp.float32),
    )
    own_full = tuple(
        (
            jnp.concatenate(
                [pad, item.transpose(1, 2, 0, 3).reshape(heads, group, rolls * span)], axis=-1
            )
            for pad, item in zip(pad_rows, own_stats)
        )
    )
    high, summed = combine_stats(prompt_stats, own_full)
    logsum = high + jnp.log(summed)
    own_logsum = logsum[:, :, block:].reshape(heads, group, rolls, span).transpose(2, 0, 1, 3)
    prompt_delta = delta_piece(
        jnp.zeros((heads, group, rows), jnp.float32),
        all_keys,
        all_values,
        queries,
        grads_out,
        qpos,
        logsum,
        scale,
    )

    def self_delta(q_one, do_one, k_one, v_one, ok_one, lse_one):
        return delta_block(q_one, do_one, k_one, v_one, ok_one[None, None], lse_one, scale)

    own_delta_part = jax.vmap(self_delta)(own_q, own_do, own_k, own_v, self_ok, own_logsum)
    own_delta_full = jnp.concatenate(
        [
            jnp.zeros((heads, group, block), jnp.float32),
            own_delta_part.transpose(1, 2, 0, 3).reshape(heads, group, rolls * span),
        ],
        axis=-1,
    )
    delta = prompt_delta + own_delta_full
    zero_buffer = jnp.zeros((total, kl_width), jnp.float32)
    start_grads = (
        jnp.zeros((rows, heads, group, width), jnp.float32),
        zero_buffer,
        zero_buffer,
        zero_buffer,
        zero_buffer,
    )
    grads = grads_piece(
        start_grads, whole, 0, queries, grads_out, qpos, logsum, delta, scale, block
    )
    dquery, dk_suffix, dv_suffix, dk_prompt, dv_prompt = grads
    summed_k, summed_v = (
        lax.psum_scatter(dk_suffix + dk_prompt, "roll", scatter_dimension=0, tiled=True),
        lax.psum_scatter(dv_suffix + dv_prompt, "roll", scatter_dimension=0, tiled=True),
    )
    own_delta = delta[:, :, block:].reshape(heads, group, rolls, span).transpose(2, 0, 1, 3)

    def self_grads(q_one, do_one, k_one, v_one, ok_one, lse_one, delta_one):
        dscore, probh, dq_part = grads_block(
            q_one, do_one, k_one, v_one, ok_one[None, None], lse_one, delta_one, scale
        )
        dk_part = jnp.einsum("kgrn,rkgd->nkd", dscore, q_one, preferred_element_type=jnp.float32)
        dv_part = jnp.einsum("kgrn,rkgd->nkd", probh, do_one, preferred_element_type=jnp.float32)
        return (dq_part, dk_part, dv_part)

    dq_self, dk_self, dv_self = jax.vmap(self_grads)(
        own_q, own_do, own_k, own_v, self_ok, own_logsum, own_delta
    )
    suffix_total = dquery[block:].reshape(rolls, span, heads, group, width) + dq_self
    suffix_dq = (
        (suffix_total * scale).astype(jnp.bfloat16).reshape(rolls, span, heads * group * width)
    )
    prompt_dq = (dquery[:block] * scale).astype(jnp.bfloat16).reshape(block, heads * group * width)
    suffix_dk = (dk_self * scale).astype(jnp.bfloat16).reshape(rolls, span, kl_width)
    suffix_dv = dv_self.astype(jnp.bfloat16).reshape(rolls, span, kl_width)
    prompt_dk = (summed_k * scale).astype(jnp.bfloat16)
    prompt_dv = summed_v.astype(jnp.bfloat16)
    part_k = lax.dot_general(
        prompt_dk, key_weight, (((1,), (1,)), ((), ())), preferred_element_type=jnp.float32
    )
    part_v = lax.dot_general(
        prompt_dv, value_weight, (((1,), (1,)), ((), ())), preferred_element_type=jnp.float32
    )
    input_grad = lax.psum_scatter(part_k + part_v, "kv", scatter_dimension=0, tiled=True).astype(
        jnp.bfloat16
    )
    return (prompt_dq, prompt_dk, prompt_dv, suffix_dq, suffix_dk, suffix_dv, input_grad)


def solution(mesh):
    placed = (
        P("roll", "kv"),
        P("roll", "kv"),
        P("roll", "kv"),
        P("roll", "kv"),
        P("roll", None, "kv"),
        P("roll", None, "kv"),
        P("roll", None, "kv"),
        P("roll", None, "kv"),
        P("roll"),
        P(None, "kv"),
        P(None, "kv"),
    )
    return jax.shard_map(
        body,
        mesh=mesh,
        in_specs=placed,
        out_specs=(
            P("roll", "kv"),
            P("roll", "kv"),
            P("roll", "kv"),
            P("roll", None, "kv"),
            P("roll", None, "kv"),
            P("roll", None, "kv"),
            P(("roll", "kv"), None),
        ),
        check_vma=False,
    )
```

profile of v0, /device:TPU:32, one launch (start us, length us, event | category | flops | bytes accessed | tf_op | source)
XLA Modules:
  0.0 523.1 jit_solution(7156123135190548323)
XLA Ops:
  11.1 39.0 %all_gather.6 = bf16[2048,128]{1,0:T(8,128)(2,1)} all-gather(bf16[64,128]{1,0:T(8,128)(2,1)} %param.18), channel_id=1, replica_groups=mesh['roll'=32,'kv'=8] {'roll'}, dimensions={0}, use_global_device_ids=true | all-gather | bytes 540672 | tf_op jit(solution)/shard_map/all_gather | solution.py:194
  50.1 35.0 %all_gather.7 = bf16[2048,128]{1,0:T(8,128)(2,1)} all-gather(bf16[64,128]{1,0:T(8,128)(2,1)} %param.19), channel_id=1, replica_groups=mesh['roll'=32,'kv'=8] {'roll'}, dimensions={0}, use_global_device_ids=true | all-gather | bytes 540672 | tf_op jit(solution)/shard_map/all_gather | solution.py:195
  95.8 16.4 %while.52 = (s32[]{:T(128)}, f32[1,8,320]{2,1,0:T(8,128)S(1)}, f32[1,8,320]{2,1,0:T(8,128)S(1)}, s32[320]{0:T(512)S(1)}, bf16[2048,128]{1,0:T(8,128)(2,1)}, /*in...) while((s32[]{:T(128)}, f32[1,8,320]{2,1,0:T(8,128)S(1)}, ...), condition=%wide.region_3.4_spmd.clone, body=%wide.region_0.3_spmd.clone.sunk | while | flops 344896512 | bytes 11902382 | solution.py:72
  115.7 20.3 %while.53 = (s32[]{:T(128)}, f32[1,8,320]{2,1,0:T(8,128)S(1)}, s32[320]{0:T(512)S(1)}, bf16[2048,128]{1,0:T(8,128)(2,1)}, bf16[320,1,8,128]{3,0,2,1:T(8,128)(2,1...) while((s32[]{:T(128)}, f32[1,8,320]{2,1,0:T(8,128)S(1)}, ...), condition=%wide.region_8.9_spmd.clone, body=%wide.region_6.8_spmd.clone.sunk | while | flops 677809152 | bytes 12443073 | solution.py:89
  117.6 3.1 fusion.145
  122.7 3.1 fusion.145
  127.8 3.1 fusion.145
  132.9 3.1 fusion.145
  136.0 3.7 fusion.62
  144.0 50.0 %while.54 = (s32[]{:T(128)}, f32[320,1,8,128]{3,0,2,1:T(8,128)}, f32[2048,128]{1,0:T(8,128)}, f32[2048,128]{1,0:T(8,128)}, f32[2048,128]{1,0:T(8,128)}, /*index=...) while((s32[]{:T(128)}, f32[320,1,8,128]{3,0,2,1:T(8,128)}, ...), condition=%wide.region_11.12_spmd.clone, body=%wide.region_10.11_spmd.clone.sunk | while | flops 1691648512 | bytes 41291316 | solution.py:148
  144.1 2.3 fusion.154
  146.4 2.8 fusion.155
  156.6 2.3 fusion.154
  158.9 2.8 fusion.155
  171.4 2.8 fusion.155
  183.9 2.8 fusion.155
  193.9 2.8 add.203
  196.8 2.3 add.204
  199.4 107.2 %reduce-scatter.4.cloned.1.call-done = f32[64,128]{1,0:T(8,128)} async-done(((f32[2048,128]{1,0:T(8,128)}), f32[64,128]{1,0:T(8,128)}) %reduce-scatter.4.cloned.1.call-update) | async-done | bytes 32784 | tf_op jit(solution)/shard_map/reduce_scatter | solution.py:266
  309.5 114.5 %reduce-scatter.6.cloned.1.call-done = f32[64,128]{1,0:T(8,128)} async-done(((f32[2048,128]{1,0:T(8,128)}), f32[64,128]{1,0:T(8,128)}) %reduce-scatter.6.cloned.1.call-update) | async-done | bytes 32784 | tf_op jit(solution)/shard_map/reduce_scatter | solution.py:267
  424.8 4.4 convolution_add_fusion
  433.1 3.0 copy.45
  438.0 2.9 fusion.82
  446.3 68.7 %reduce-scatter.8.cloned.1.call-done = f32[8,8192]{1,0:T(8,128)} async-done(((f32[64,8192]{1,0:T(8,128)}), f32[8,8192]{1,0:T(8,128)}) %reduce-scatter.8.cloned.1.call-update) | async-done | bytes 262160 | tf_op jit(solution)/shard_map/reduce_scatter | solution.py:297
  (158 shorter events, 95.7 us)
Async XLA Ops:
  7.2 300.2 %copy-start = (bf16[8192,128]{1,0:T(8,128)(2,1)S(1)}, bf16[8192,128]{1,0:T(8,128)(2,1)}, u32[]{:S(2)}) copy-start(bf16[8192,128]{1,0:T(8,128)(2,1)} %param.26) | copy-start | bytes 6291460
  7.2 77.9 %copy-start.8 = (bf16[1,256,1024]{2,1,0:T(8,128)(2,1)S(1)}, bf16[1,256,1024]{2,1,0:T(8,128)(2,1)}, u32[]{:S(2)}) copy-start(bf16[1,256,1024]{2,1,0:T(8,128)(2,1)} %param.24) | copy-start | bytes 1572868
  7.2 299.4 %reduce-scatter.4.cloned.1.call-start = ((), (), s32[]{:S(2)}) async-start(), calls=%async_computation.3 | async-start | bytes 1081344 | tf_op jit(solution)/shard_map/reduce_scatter | solution.py:266
  85.3 0.8 copy-start.4
  113.8 1.3 copy-start.3
  150.3 1.4 copy-start.1
  153.8 2.6 copy-start.2
  162.8 1.5 copy-start.1
  166.3 2.6 copy-start.2
  175.3 1.5 copy-start.1
  178.8 2.6 copy-start.2
  187.8 1.5 copy-start.1
  191.3 2.6 copy-start.2
  193.9 2.8 copy-start.7
  196.7 227.3 %reduce-scatter.6.cloned.1.call-start = ((), (), s32[]{:S(2)}) async-start(), calls=%async_computation.4 | async-start | bytes 1081344 | tf_op jit(solution)/shard_map/reduce_scatter | solution.py:267
  199.1 315.9 %reduce-scatter.8.cloned.1.call-start = ((), (), s32[]{:S(2)}) async-start(), calls=%async_computation.5 | async-start | bytes 2359296 | tf_op jit(solution)/shard_map/reduce_scatter | solution.py:297
  307.3 2.2 copy-start.10
  424.8 4.4 copy-start.11
  429.2 1.0 copy-start.5
  438.0 2.9 copy-start.6
  438.0 2.9 copy-start.9
Sparse Core Ops, SparseCore 0:
  196.8 109.6 reduce-scatter.3
  309.2 114.7 reduce-scatter.5
  429.3 85.5 reduce-scatter.7
where the time goes:
time: 524 us; the launch traced here: 523 us
  waiting for transfers between devices  290 us (55%)
  matrix products  93.7 us (18%)
  blocking collectives  74 us (14%)
  other arithmetic  25.7 us (5%)
  local copies, waits for them, and re-layouts  23.3 us (4%)
  between operations  14.8 us (3%)
    reduce_scatter x1, waiting for transfers between devices, body(): lax.psum_scatter(dv_suffix + dv_prompt, 'roll', scatter_dimension=0, tile...  115 us
    reduce_scatter x1, waiting for transfers between devices, body(): lax.psum_scatter(dk_suffix + dk_prompt, 'roll', scatter_dimension=0, tile...  107 us
    reduce_scatter x1, waiting for transfers between devices, body(): lax.psum_scatter(part_k + part_v, 'kv', scatter_dimension=0, tiled=True)  68.7 us
    all_gather x1, blocking collectives, body(): lax.all_gather(prompt_k, 'roll', axis=0, tiled=True)  39 us
    all_gather x1, blocking collectives, body(): lax.all_gather(prompt_v, 'roll', axis=0, tiled=True)  35 us
    unnamed x28, local copies, waits for them, and re-layouts  13 us
    dot_general x4, matrix products, delta_block(): jnp.einsum('rkgd,nkd->kgrn', queries, kblk, preferred_element_type=jnp.fl...  12.4 us
    dot_general x4, matrix products, probs_block(): jnp.einsum('rkgd,nkd->kgrn', grads_out, vblk, preferred_element_type=jnp....  11.3 us
  transfers between devices with their start and end apart: 3, of which 3 were waited for; matrix products, arithmetic and copies ran while one was open for 4% of the time, Pallas kernels for 0%

commit v1 on v0

v1 whole, which is shorter than its diff:
```python
import functools

import jax
import jax.numpy as jnp
from jax import lax
from jax.experimental import pallas as pl
from jax.experimental.pallas import tpu as pltpu
from jax.sharding import PartitionSpec as P

F32 = jnp.float32
BF = jnp.bfloat16
HD = 128
HEADS = 8
PR = 64
SR = 256
ROLL = 32
KEYS = 2048
CK = 256
SCALE = HD**-0.5
ALPHA = SCALE * 1.4426950408889634
NEG = -1e30
NT = (((1,), (1,)), ((), ()))
NN = (((1,), (0,)), ((), ()))
MESH = pl.DeviceIdType.MESH
D = 8192
NCOL = 4
CW = D // 2 // NCOL
HW = CW // 2


def dot(a, b, dims):
    return lax.dot_general(a, b, dims, preferred_element_type=F32)


def fold(x, op):
    return op(x.reshape(x.shape[0] // 8, 8, x.shape[1]), axis=0)


def body_kernel(
    pq, pk, pv, pdo, sq, sk, sv, sdo, ln, kw_hbm, vw_hbm,
    o_pdq, o_pdk, o_pdv, o_sdq, o_sdk, o_sdv, o_in,
    kv, kt, q, do, ex, dsc, dp_s, s_s, kw, vw,
    a_send, a_keep, a_recv, b_send, b_keep, b_recv, c_send, c_recv,
    part, x1_send, x1_recv, x2_send, x2_recv, y_keep, y_send, y_recv,
    loc, ag_s, ag_r, a_ss, a_rs, b_ss, b_rs, c_ss, c_rs,
    x1_ss, x1_rs, x2_ss, x2_rs, y_ss, y_rs,
):
    roll = lax.axis_index("roll")
    grp = lax.axis_index("kv")
    z = roll // 4
    y = (roll // 2) % 2
    c = roll % 2
    yh = grp // 4
    x = grp % 4

    def rdev(zz, yy, cc):
        return (zz * 4 + yy * 2 + cc, grp)

    def kdev(hh, xx):
        return (roll, hh * 4 + xx)

    sib = rdev(z, y, 1 - c)
    ypar = rdev(z, 1 - y, c)
    xp = kdev(yh, (x + 1) % 4)
    xm = kdev(yh, (x + 3) % 4)
    hpar = kdev(1 - yh, x)

    copies = []

    def local(src, dst):
        cp = pltpu.make_async_copy(src, dst, loc.at[len(copies)])
        cp.start()
        copies.append(cp)

    local(pk, kv.at[roll, 0])
    local(pv, kv.at[roll, 1])
    for h in range(HEADS):
        cols = slice(h * HD, (h + 1) * HD)
        local(sq.at[0, :, cols], q.at[h * SR : (h + 1) * SR, :])
        local(sdo.at[0, :, cols], do.at[h * SR : (h + 1) * SR, :])
        base = HEADS * SR + h * PR
        local(pq.at[:, cols], q.at[base : base + PR, :])
        local(pdo.at[:, cols], do.at[base : base + PR, :])
    for i in range(4):
        local(sk.at[0, i * PR : (i + 1) * PR, :], kv.at[ROLL + i, 0])
        local(sv.at[0, i * PR : (i + 1) * PR, :], kv.at[ROLL + i, 1])
    local(kw_hbm, kw)
    local(vw_hbm, vw)

    barrier = pltpu.get_barrier_semaphore()
    peers = [rdev((z + d) % 8, y, c) for d in range(1, 8)] + [sib, ypar, xp, xm, hpar]
    for peer in peers:
        pl.semaphore_signal(barrier, inc=1, device_id=peer, device_id_type=MESH)
    pl.semaphore_wait(barrier, len(peers))

    def gather_copy(block, peer, slot):
        return pltpu.make_async_remote_copy(
            src_ref=kv.at[block], dst_ref=kv.at[block],
            send_sem=ag_s.at[slot], recv_sem=ag_r.at[block],
            device_id=peer, device_id_type=MESH,
        )

    sends = []

    def push(block, peer):
        cp = gather_copy(block, peer, len(sends))
        cp.start()
        sends.append(cp)

    copies[0].wait()
    copies[1].wait()
    order = (1, 7, 2, 6, 3, 5, 4)
    for d in order:
        push(roll, rdev((z + d) % 8, y, c))
    push(roll, ypar)
    push(roll, sib)
    for d in order:
        src = ((z + 8 - d) % 8) * 4 + y * 2 + c
        gather_copy(src, sib, 0).wait_recv()
        push(src, ypar)
        push(src, sib)
    for d in (0,) + order:
        src = ((z + 8 - d) % 8) * 4 + (1 - y) * 2 + c
        gather_copy(src, sib, 0).wait_recv()
        push(src, sib)
    for cp in copies[2:-2]:
        cp.wait()
    for d in (0,) + order:
        for yy in range(2):
            src = ((z + 8 - d) % 8) * 4 + yy * 2 + 1 - c
            gather_copy(src, sib, 0).wait_recv()
    for cp in sends:
        cp.wait_send()

    def keys(i):
        return kv[4 * i : 4 * i + 4, 0].reshape(CK, HD)

    def values(i):
        return kv[4 * i : 4 * i + 4, 1].reshape(CK, HD)

    n_live = ln[0]
    for i in range(9):
        kt[:, i * CK : (i + 1) * CK] = keys(i).T
    live = lax.broadcasted_iota(jnp.int32, (SR, HD), 0) < n_live
    for h in range(HEADS):
        rows = slice(h * SR, (h + 1) * SR)
        do[rows, :] = jnp.where(live, do[rows, :], jnp.zeros((), BF))
    kpos = lax.broadcasted_iota(jnp.int32, (CK, SR), 0)
    qpos = lax.broadcasted_iota(jnp.int32, (CK, SR), 1)

    def own_mask(i, s):
        if i < 8:
            return s
        return jnp.where((kpos <= qpos) & (kpos < n_live), s, NEG)

    def causal_mask(i, s):
        return jnp.where(kpos + i * CK <= roll * PR + (qpos & (PR - 1)), s, NEG)

    def tile(t, chunks, mask):
        r0 = pl.multiple_of(t * SR, SR)
        cols = pl.ds(r0, SR)
        qt = q[cols, :]
        dt = do[cols, :]
        top = jnp.full((8, SR), NEG, F32)
        for i in range(chunks):
            s = mask(i, dot(keys(i), qt, NT))
            s_s[i * CK : (i + 1) * CK, :] = s
            top = jnp.maximum(top, fold(s, jnp.max))
        top = jnp.max(top, axis=0, keepdims=True) * ALPHA
        total = jnp.zeros((8, SR), F32)
        delta = jnp.zeros((8, SR), F32)
        for i in range(chunks):
            rows = slice(i * CK, (i + 1) * CK)
            e = jnp.exp2(s_s[rows, :] * ALPHA - top)
            dp = dot(values(i), dt, NT)
            total = total + fold(e, jnp.sum)
            delta = delta + fold(e * dp, jnp.sum)
            ex[rows, cols] = e.astype(BF)
            dp_s[rows, :] = dp
        inv = 1.0 / jnp.sum(total, axis=0, keepdims=True)
        delta = jnp.sum(delta, axis=0, keepdims=True) * inv
        acc = jnp.zeros((HD, SR), F32)
        for i in range(chunks):
            rows = slice(i * CK, (i + 1) * CK)
            ds = (ex[rows, cols].astype(F32) * (dp_s[rows, :] - delta)).astype(BF)
            dsc[rows, cols] = ds
            acc = acc + dot(kt[:, rows], ds, NN)
        invc = jnp.broadcast_to(inv, (HD, SR)).T
        q[cols, :] = (qt.astype(F32) * invc).astype(BF)
        do[cols, :] = (dt.astype(F32) * invc).astype(BF)
        return (acc * (inv * SCALE)).T.astype(BF)

    def roll_tile(t, carry):
        o_sdq[0, :, pl.ds(pl.multiple_of(t * HD, HD), HD)] = tile(t, 9, own_mask)
        return carry

    lax.fori_loop(0, HEADS, roll_tile, 0)

    def prompt_tile(t, carry):
        dq = tile(t, 8, causal_mask)
        for h in range(4):
            col = pl.multiple_of(((t - HEADS) * 4 + h) * HD, HD)
            o_pdq[:, pl.ds(col, HD)] = dq[h * PR : (h + 1) * PR, :]
        return carry

    lax.fori_loop(HEADS, HEADS + 2, prompt_tile, 0)

    own = slice(KEYS, KEYS + SR)
    live_rows = HEADS * SR

    def zoff(i):
        return (z + 4 + (1 - 2 * (i % 2)) * ((i + 1) // 2)) % 8

    def a_copy(i):
        return pltpu.make_async_remote_copy(
            src_ref=a_send.at[i], dst_ref=a_recv.at[i], send_sem=a_ss.at[i],
            recv_sem=a_rs.at[i], device_id=sib, device_id_type=MESH,
        )

    def b_copy(i):
        return pltpu.make_async_remote_copy(
            src_ref=b_send.at[i], dst_ref=b_recv.at[i], send_sem=b_ss.at[i],
            recv_sem=b_rs.at[i], device_id=ypar, device_id_type=MESH,
        )

    def c_copy(i, slot, zz):
        return pltpu.make_async_remote_copy(
            src_ref=c_send.at[i], dst_ref=c_recv.at[slot], send_sem=c_ss.at[i],
            recv_sem=c_rs.at[slot], device_id=rdev(zz, y, c), device_id_type=MESH,
        )

    first_core = c == 0
    first_y = y == 0

    def compute(i):
        k0 = pl.multiple_of(zoff(i) * CK, CK)
        dk = dot(dsc[pl.ds(k0, CK), :], q[...], NN)
        dv = dot(ex[pl.ds(k0, CK), :], do[...], NN)
        for yy in range(2):
            lo = slice(yy * 2 * PR, yy * 2 * PR + PR)
            hi = slice(yy * 2 * PR + PR, yy * 2 * PR + 2 * PR)
            for part_, g in ((0, dk), (1, dv)):
                col = slice(part_ * HD, (part_ + 1) * HD)
                a_keep[i, yy, :, col] = jnp.where(first_core, g[lo], g[hi])
                a_send[i, yy, :, col] = jnp.where(first_core, g[hi], g[lo]).astype(BF)
        a_copy(i).start()

    def after_a(i):
        a_copy(i).wait_recv()
        s0 = a_keep[i, 0] + a_recv[i, 0].astype(F32)
        s1 = a_keep[i, 1] + a_recv[i, 1].astype(F32)
        b_keep[i] = jnp.where(first_y, s0, s1)
        b_send[i] = jnp.where(first_y, s1, s0).astype(BF)
        b_copy(i).start()

    def after_b(i):
        b_copy(i).wait_recv()
        return b_keep[i] + b_recv[i].astype(F32)

    def send_c(i):
        c_send[i] = after_b(i).astype(BF)
        c_copy(i, z, zoff(i)).start()

    def grads(i, carry):
        compute(i)

        @pl.when(i >= 1)
        def _():
            after_a(i - 1)

        @pl.when(i >= 2)
        def _():
            send_c(i - 2)

        return carry

    lax.fori_loop(0, 8, grads, 0)
    after_a(7)
    send_c(6)
    o_sdv[0] = dot(ex[own, 0:live_rows], do[0:live_rows, :], NN).astype(BF)
    o_sdk[0] = (dot(dsc[own, 0:live_rows], q[0:live_rows, :], NN) * SCALE).astype(BF)
    summed = after_b(7)
    for d in (1, 7, 2, 6, 3, 5, 4):
        slot = (z + d) % 8
        c_copy(0, slot, slot).wait_recv()
        summed = summed + c_recv[slot].astype(F32)
    dk = (summed[:, :HD] * SCALE).astype(BF)
    dv = summed[:, HD:].astype(BF)
    o_pdk[...] = dk
    o_pdv[...] = dv
    for i in range(8):
        a_copy(i).wait_send()
        b_copy(i).wait_send()
    for i in range(7):
        c_copy(i, z, zoff(i)).wait_send()
    copies[-2].wait()
    copies[-1].wait()

    def x_copy(send, recv, ss, rs, k, side):
        return pltpu.make_async_remote_copy(
            src_ref=send.at[k, side], dst_ref=recv.at[k, side], send_sem=ss.at[k, side],
            recv_sem=rs.at[k, side], device_id=(xp, xm)[side], device_id_type=MESH,
        )

    def y_copy(k):
        return pltpu.make_async_remote_copy(
            src_ref=y_send.at[k], dst_ref=y_recv.at[k], send_sem=y_ss.at[k],
            recv_sem=y_rs.at[k], device_id=hpar, device_id_type=MESH,
        )

    def piece(k, hh, xx, cols):
        r0 = pl.multiple_of((hh * 4 + xx) * 8, 8)
        return jnp.concatenate(
            [part[k, 0, pl.ds(r0, 8), cols], part[k, 1, pl.ds(r0, 8), cols]], axis=0
        )

    halves = (slice(0, HW), slice(HW, CW))
    ahead = ((x + 1) % 4, (x + 3) % 4)
    far = (x + 2) % 4

    for k in range(NCOL):
        for half in range(2):
            rows = slice(half * (D // 2) + k * CW, half * (D // 2) + (k + 1) * CW)
            part[k, half] = dot(dk, kw[rows, :], NT) + dot(dv, vw[rows, :], NT)
        for side in range(2):
            for hh in range(2):
                x1_send[k, side, 0, hh] = piece(k, hh, far, halves[side]).astype(BF)
                x1_send[k, side, 1, hh] = piece(k, hh, ahead[side], halves[1 - side]).astype(BF)
            x_copy(x1_send, x1_recv, x1_ss, x1_rs, k, side).start()
    for k in range(NCOL):
        for side in range(2):
            x_copy(x1_send, x1_recv, x1_ss, x1_rs, k, side).wait_recv()
            for hh in range(2):
                mine = piece(k, hh, ahead[side], halves[side])
                x2_send[k, side, hh] = (mine + x1_recv[k, side, 0, hh].astype(F32)).astype(BF)
            x_copy(x2_send, x2_recv, x2_ss, x2_rs, k, side).start()
    for k in range(NCOL):
        for side in range(2):
            x_copy(x2_send, x2_recv, x2_ss, x2_rs, k, side).wait_recv()
        for half in range(2):
            def gathered(hh):
                return (
                    piece(k, hh, x, halves[half])
                    + x2_recv[k, half, hh].astype(F32)
                    + x1_recv[k, 1 - half, 1, hh].astype(F32)
                )

            y_keep[k, :, halves[half]] = gathered(yh)
            y_send[k, :, halves[half]] = gathered(1 - yh).astype(BF)
        y_copy(k).start()
    for k in range(NCOL):
        y_copy(k).wait_recv()
        full = y_keep[k] + y_recv[k].astype(F32)
        o_in[:, k * CW : (k + 1) * CW] = full[0:8].astype(BF)
        o_in[:, D // 2 + k * CW : D // 2 + (k + 1) * CW] = full[8:16].astype(BF)
    for k in range(NCOL):
        for side in range(2):
            x_copy(x1_send, x1_recv, x1_ss, x1_rs, k, side).wait_send()
            x_copy(x2_send, x2_recv, x2_ss, x2_rs, k, side).wait_send()
        y_copy(k).wait_send()


def body(*args):
    anyspec = pl.BlockSpec(memory_space=pl.ANY)
    vspec = pl.BlockSpec(memory_space=pltpu.VMEM)
    sspec = pl.BlockSpec(memory_space=pltpu.SMEM)
    shape = jax.ShapeDtypeStruct
    dma = pltpu.SemaphoreType.DMA
    rows = HEADS * (SR + PR)
    return pl.pallas_call(
        body_kernel,
        in_specs=[anyspec] * 8 + [sspec] + [anyspec] * 2,
        out_specs=[vspec] * 7,
        out_shape=[
            shape((PR, HEADS * HD), BF),
            shape((PR, HD), BF),
            shape((PR, HD), BF),
            shape((1, SR, HEADS * HD), BF),
            shape((1, SR, HD), BF),
            shape((1, SR, HD), BF),
            shape((8, D), BF),
        ],
        scratch_shapes=[
            pltpu.VMEM((ROLL + 4, 2, PR, HD), BF),
            pltpu.VMEM((HD, KEYS + SR), BF),
            pltpu.VMEM((rows, HD), BF),
            pltpu.VMEM((rows, HD), BF),
            pltpu.VMEM((KEYS + SR, rows), BF),
            pltpu.VMEM((KEYS + SR, rows), BF),
            pltpu.VMEM((KEYS + SR, SR), F32),
            pltpu.VMEM((KEYS + SR, SR), F32),
            pltpu.VMEM((D, HD), BF),
            pltpu.VMEM((D, HD), BF),
            pltpu.VMEM((8, 2, PR, 2 * HD), BF),
            pltpu.VMEM((8, 2, PR, 2 * HD), F32),
            pltpu.VMEM((8, 2, PR, 2 * HD), BF),
            pltpu.VMEM((8, PR, 2 * HD), BF),
            pltpu.VMEM((8, PR, 2 * HD), F32),
            pltpu.VMEM((8, PR, 2 * HD), BF),
            pltpu.VMEM((8, PR, 2 * HD), BF),
            pltpu.VMEM((8, PR, 2 * HD), BF),
            pltpu.VMEM((NCOL, 2, 64, CW), F32),
            pltpu.VMEM((NCOL, 2, 2, 2, 16, HW), BF),
            pltpu.VMEM((NCOL, 2, 2, 2, 16, HW), BF),
            pltpu.VMEM((NCOL, 2, 2, 16, HW), BF),
            pltpu.VMEM((NCOL, 2, 2, 16, HW), BF),
            pltpu.VMEM((NCOL, 16, CW), F32),
            pltpu.VMEM((NCOL, 16, CW), BF),
            pltpu.VMEM((NCOL, 16, CW), BF),
            dma((44,)),
            dma((31,)),
            dma((32,)),
            dma((8,)),
            dma((8,)),
            dma((8,)),
            dma((8,)),
            dma((8,)),
            dma((8,)),
            dma((NCOL, 2)),
            dma((NCOL, 2)),
            dma((NCOL, 2)),
            dma((NCOL, 2)),
            dma((NCOL,)),
            dma((NCOL,)),
        ],
        compiler_params=pltpu.CompilerParams(
            collective_id=0, has_side_effects=True, vmem_limit_bytes=60 * 1024 * 1024
        ),
    )(*args)


def solution(mesh):
    placed = (
        P("roll", "kv"),
        P("roll", "kv"),
        P("roll", "kv"),
        P("roll", "kv"),
        P("roll", None, "kv"),
        P("roll", None, "kv"),
        P("roll", None, "kv"),
        P("roll", None, "kv"),
        P("roll"),
        P(None, "kv"),
        P(None, "kv"),
    )
    return jax.shard_map(
        lambda *args: tuple(body(*args)),
        mesh=mesh,
        in_specs=placed,
        out_specs=(
            P("roll", "kv"),
            P("roll", "kv"),
            P("roll", "kv"),
            P("roll", None, "kv"),
            P("roll", None, "kv"),
            P("roll", None, "kv"),
            P(("roll", "kv"), None),
        ),
        check_vma=False,
    )
```

time: 524 us -> 90.2 us (0.17)
  waiting for transfers between devices: 290 us -> 0 us
  matrix products: 93.7 us -> 0 us
  Pallas kernels: 0 us -> 77.6 us
  blocking collectives: 74 us -> 0 us
  other arithmetic: 25.7 us -> 0 us
  between operations: 14.8 us -> 1.29 us
  local copies, waits for them, and re-layouts: 23.3 us -> 10.6 us
    reduce_scatter x3 -> x0, waiting for transfers between devices: 290 us -> none  [the longest x1 115 us: body(): lax.psum_scatter(dv_suffix + dv_prompt, 'roll', scatter_dimension=0, tile...]
    dot_general x47 -> x0, matrix products: 93.7 us -> none  [the longest x4 12.4 us: delta_block(): jnp.einsum('rkgd,nkd->kgrn', queries, kblk, preferred_element_type=jnp.fl...]
    pallas_call x0 -> x1, Pallas kernels: none -> 77.6 us  [body(): pl.pallas_call(body_kernel, in_specs=[anyspec] * 8 + [sspec] + [anyspec]...]
    all_gather x2 -> x0, blocking collectives: 74 us -> none  [the longest x1 39 us: body(): lax.all_gather(prompt_k, 'roll', axis=0, tiled=True)]
    reduce_sum x5 -> x0, other arithmetic: 7.78 us -> none  [stats_block(): return (new_high, total * factor + jnp.sum(expo, axis=-1))]
    add x26 -> x0, other arithmetic: 5.36 us -> none  [the longest x1 2.77 us: body(): dk_suffix + dk_prompt]
    unnamed x28 -> x7, local copies, waits for them, and re-layouts: 13 us -> 10.6 us
  transfers between devices with their start and end apart: 3 -> 0, of which waited for: 3 -> 0; matrix products, arithmetic and copies ran while one was open for 4% -> 0% of each run, Pallas kernels for 0% -> 0%
where the time goes in v1:
time: 90.2 us; the launch traced here: 89.5 us
  Pallas kernels  77.6 us (86%)
  local copies, waits for them, and re-layouts  10.6 us (12%)
  between operations  1.29 us (1%)
    pallas_call x1, Pallas kernels, body(): pl.pallas_call(body_kernel, in_specs=[anyspec] * 8 + [sspec] + [anyspec]...  77.6 us
    unnamed x7, local copies, waits for them, and re-layouts  10.6 us

profile of v1, /device:TPU:32, one launch (start us, length us, event | category | flops | bytes accessed | tf_op | source)
XLA Modules:
  0.0 89.5 jit_solution(3795119031090577355)
XLA Ops:
  1.3 77.6 %shard_map.162 = (bf16[64,1024]{1,0:T(8,128)(2,1)}, bf16[64,128]{1,0:T(8,128)(2,1)}, bf16[64,128]{1,0:T(8,128)(2,1)}, bf16[1,256,1024]{2,1,0:T(8,128)(2,1)}, bf1...) custom-call(bf16[64,1024]{1,0:T(8,128)(2,1)} %pq.1, bf16[64,128]{1,0:T(8,128)(2,1)} %pk.1, ...), custom_call_target="tpu_custom_call" | custom-call | tf_op jit(solution)/shard_map/pallas_call | solution.py:370
  78.9 1.6 %copy.26 = bf16[64,1024]{1,0:T(8,128)(2,1)} copy(bf16[64,1024]{1,0:T(8,128)(2,1)} %get-tuple-element.14) | data formatting | bytes 262144
  80.5 1.3 %copy.27 = bf16[64,128]{1,0:T(8,128)(2,1)} copy(bf16[64,128]{1,0:T(8,128)(2,1)} %get-tuple-element.15) | data formatting | bytes 32768
  81.8 1.3 %copy.28 = bf16[64,128]{1,0:T(8,128)(2,1)} copy(bf16[64,128]{1,0:T(8,128)(2,1)} %get-tuple-element.16) | data formatting | bytes 32768
  83.1 1.9 %copy.29 = bf16[1,256,1024]{2,1,0:T(8,128)(2,1)} copy(bf16[1,256,1024]{2,1,0:T(8,128)(2,1)} %get-tuple-element.17) | data formatting | bytes 1048576
  85.0 1.5 %copy.30 = bf16[1,256,128]{2,1,0:T(8,128)(2,1)} copy(bf16[1,256,128]{2,1,0:T(8,128)(2,1)} %get-tuple-element.18) | data formatting | bytes 131072
  86.5 1.5 %copy.31 = bf16[1,256,128]{2,1,0:T(8,128)(2,1)} copy(bf16[1,256,128]{2,1,0:T(8,128)(2,1)} %get-tuple-element.19) | data formatting | bytes 131072
  88.0 1.6 %copy.32 = bf16[8,8192]{1,0:T(8,128)(2,1)} copy(bf16[8,8192]{1,0:T(8,128)(2,1)} %get-tuple-element.20) | data formatting | bytes 262144

commit v2 on v1

--- a/solution.py
+++ b/solution.py
@@ -156,7 +156,7 @@
     def causal_mask(i, s):
         return jnp.where(kpos + i * CK <= roll * PR + (qpos & (PR - 1)), s, NEG)
 
-    def tile(t, chunks, mask):
+    def tile(t, slot, chunks, mask, finish):
         r0 = pl.multiple_of(t * SR, SR)
         cols = pl.ds(r0, SR)
         qt = q[cols, :]
@@ -164,46 +164,59 @@
         top = jnp.full((8, SR), NEG, F32)
         for i in range(chunks):
             s = mask(i, dot(keys(i), qt, NT))
-            s_s[i * CK : (i + 1) * CK, :] = s
+            s_s[slot, i * CK : (i + 1) * CK, :] = s
             top = jnp.maximum(top, fold(s, jnp.max))
+        yield
         top = jnp.max(top, axis=0, keepdims=True) * ALPHA
         total = jnp.zeros((8, SR), F32)
         delta = jnp.zeros((8, SR), F32)
         for i in range(chunks):
             rows = slice(i * CK, (i + 1) * CK)
-            e = jnp.exp2(s_s[rows, :] * ALPHA - top)
+            e = jnp.exp2(s_s[slot, rows, :] * ALPHA - top)
             dp = dot(values(i), dt, NT)
             total = total + fold(e, jnp.sum)
             delta = delta + fold(e * dp, jnp.sum)
-            ex[rows, cols] = e.astype(BF)
-            dp_s[rows, :] = dp
+            s_s[slot, rows, :] = e
+            dp_s[slot, rows, :] = dp
         inv = 1.0 / jnp.sum(total, axis=0, keepdims=True)
         delta = jnp.sum(delta, axis=0, keepdims=True) * inv
+        yield
         acc = jnp.zeros((HD, SR), F32)
         for i in range(chunks):
             rows = slice(i * CK, (i + 1) * CK)
-            ds = (ex[rows, cols].astype(F32) * (dp_s[rows, :] - delta)).astype(BF)
+            p = s_s[slot, rows, :] * inv
+            ds = (p * (dp_s[slot, rows, :] - delta)).astype(BF)
+            ex[rows, cols] = p.astype(BF)
             dsc[rows, cols] = ds
             acc = acc + dot(kt[:, rows], ds, NN)
-        invc = jnp.broadcast_to(inv, (HD, SR)).T
-        q[cols, :] = (qt.astype(F32) * invc).astype(BF)
-        do[cols, :] = (dt.astype(F32) * invc).astype(BF)
-        return (acc * (inv * SCALE)).T.astype(BF)
-
-    def roll_tile(t, carry):
-        o_sdq[0, :, pl.ds(pl.multiple_of(t * HD, HD), HD)] = tile(t, 9, own_mask)
+        finish(t, (acc * SCALE).T.astype(BF))
+        yield
+
+    def pair(t, chunks, mask, finish):
+        tiles = [tile(2 * t + slot, slot, chunks, mask, finish) for slot in range(2)]
+        for _ in range(3):
+            for one in tiles:
+                next(one)
+
+    def roll_out(t, dq):
+        o_sdq[0, :, pl.ds(pl.multiple_of(t * HD, HD), HD)] = dq
+
+    def roll_pair(t, carry):
+        pair(t, 9, own_mask, roll_out)
         return carry
 
-    lax.fori_loop(0, HEADS, roll_tile, 0)
-
-    def prompt_tile(t, carry):
-        dq = tile(t, 8, causal_mask)
+    lax.fori_loop(0, HEADS // 2, roll_pair, 0)
+
+    def prompt_out(t, dq):
         for h in range(4):
             col = pl.multiple_of(((t - HEADS) * 4 + h) * HD, HD)
             o_pdq[:, pl.ds(col, HD)] = dq[h * PR : (h + 1) * PR, :]
+
+    def prompt_pair(t, carry):
+        pair(t, 8, causal_mask, prompt_out)
         return carry
 
-    lax.fori_loop(HEADS, HEADS + 2, prompt_tile, 0)
+    lax.fori_loop(HEADS // 2, HEADS // 2 + 1, prompt_pair, 0)
 
     own = slice(KEYS, KEYS + SR)
     live_rows = HEADS * SR
@@ -358,6 +371,29 @@
             x_copy(x1_send, x1_recv, x1_ss, x1_rs, k, side).wait_send()
             x_copy(x2_send, x2_recv, x2_ss, x2_rs, k, side).wait_send()
         y_copy(k).wait_send()
+
+
+def hand_on_kernel(*refs):
+    count = len(refs) // 2
+    copies = []
+    for i in range(count):
+        cp = pltpu.make_async_copy(refs[i], refs[count + i], refs[-1].at[i])
+        cp.start()
+        copies.append(cp)
+    for cp in copies:
+        cp.wait()
+
+
+def hand_on(arrays):
+    spec = pl.BlockSpec(memory_space=pl.ANY)
+    vspec = pl.BlockSpec(memory_space=pltpu.VMEM)
+    return pl.pallas_call(
+        hand_on_kernel,
+        in_specs=[vspec] * len(arrays),
+        out_specs=[spec] * len(arrays),
+        out_shape=[jax.ShapeDtypeStruct(a.shape, a.dtype) for a in arrays],
+        scratch_shapes=[pltpu.SemaphoreType.DMA((len(arrays),))],
+    )(*arrays)
 
 
 def body(*args):
@@ -387,8 +423,8 @@
             pltpu.VMEM((rows, HD), BF),
             pltpu.VMEM((KEYS + SR, rows), BF),
             pltpu.VMEM((KEYS + SR, rows), BF),
-            pltpu.VMEM((KEYS + SR, SR), F32),
-            pltpu.VMEM((KEYS + SR, SR), F32),
+            pltpu.VMEM((2, KEYS + SR, SR), F32),
+            pltpu.VMEM((2, KEYS + SR, SR), F32),
             pltpu.VMEM((D, HD), BF),
             pltpu.VMEM((D, HD), BF),
             pltpu.VMEM((8, 2, PR, 2 * HD), BF),
@@ -444,7 +480,7 @@
         P(None, "kv"),
     )
     return jax.shard_map(
-        lambda *args: tuple(body(*args)),
+        lambda *args: tuple(hand_on(body(*args))),
         mesh=mesh,
         in_specs=placed,
         out_specs=(

time: 90.2 us -> 76.7 us (0.85)
  local copies, waits for them, and re-layouts: 10.6 us -> 0 us
  Pallas kernels: 77.6 us -> 75 us
    unnamed x7 -> x0, local copies, waits for them, and re-layouts: 10.6 us -> none
    pallas_call x1, Pallas kernels: 77.6 us -> 72.9 us  [body(): pl.pallas_call(body_kernel, in_specs=[anyspec] * 8 + [sspec] + [anyspec]...]
    pallas_call x0 -> x1, Pallas kernels: none -> 2.16 us  [hand_on(): pl.pallas_call(hand_on_kernel, in_specs=[vspec] * len(arrays), out_specs=...]
where the time goes in v2:
time: 76.7 us; the launch traced here: 76.3 us
  Pallas kernels  75 us (98%)
  between operations  1.29 us (2%)
    pallas_call x1, Pallas kernels, body(): pl.pallas_call(body_kernel, in_specs=[anyspec] * 8 + [sspec] + [anyspec]...  72.9 us
    pallas_call x1, Pallas kernels, hand_on(): pl.pallas_call(hand_on_kernel, in_specs=[vspec] * len(arrays), out_specs=...  2.16 us

profile of v2, /device:TPU:32, one launch (start us, length us, event | category | flops | bytes accessed | tf_op | source)
XLA Modules:
  0.0 76.3 jit_solution(8576591449869492957)
XLA Ops:
  1.3 72.9 %shard_map.162 = (bf16[64,1024]{1,0:T(8,128)(2,1)}, bf16[64,128]{1,0:T(8,128)(2,1)}, bf16[64,128]{1,0:T(8,128)(2,1)}, bf16[1,256,1024]{2,1,0:T(8,128)(2,1)}, bf1...) custom-call(bf16[64,1024]{1,0:T(8,128)(2,1)} %pq.1, bf16[64,128]{1,0:T(8,128)(2,1)} %pk.1, ...), custom_call_target="tpu_custom_call" | custom-call | tf_op jit(solution)/shard_map/pallas_call | solution.py:406
  74.2 2.2 %shard_map.163 = (bf16[64,1024]{1,0:T(8,128)(2,1)}, bf16[64,128]{1,0:T(8,128)(2,1)}, bf16[64,128]{1,0:T(8,128)(2,1)}, bf16[1,256,1024]{2,1,0:T(8,128)(2,1)}, bf1...) custom-call(bf16[64,1024]{1,0:T(8,128)(2,1)} %get-tuple-element.14.refs_0_, ...), custom_call_target="tpu_custom_call" | custom-call | tf_op jit(solution)/shard_map/pallas_call | solution.py:390

commit v3 on v2

--- a/solution.py
+++ b/solution.py
@@ -12,6 +12,7 @@
 HD = 128
 HEADS = 8
 PR = 64
+HR = PR // 2
 SR = 256
 ROLL = 32
 KEYS = 2048
@@ -26,6 +27,8 @@
 NCOL = 4
 CW = D // 2 // NCOL
 HW = CW // 2
+LAG_A = 2
+LAG_B = 4
 
 
 def dot(a, b, dims):
@@ -40,7 +43,7 @@
     pq, pk, pv, pdo, sq, sk, sv, sdo, ln, kw_hbm, vw_hbm,
     o_pdq, o_pdk, o_pdv, o_sdq, o_sdk, o_sdv, o_in,
     kv, kt, q, do, ex, dsc, dp_s, s_s, kw, vw,
-    a_send, a_keep, a_recv, b_send, b_keep, b_recv, c_send, c_recv,
+    a_send, a_keep, a_recv, b_send, b_keep, b_recv, c_send, c_recv, own_keep,
     part, x1_send, x1_recv, x2_send, x2_recv, y_keep, y_send, y_recv,
     loc, ag_s, ag_r, a_ss, a_rs, b_ss, b_rs, c_ss, c_rs,
     x1_ss, x1_rs, x2_ss, x2_rs, y_ss, y_rs,
@@ -236,141 +239,180 @@
             recv_sem=b_rs.at[i], device_id=ypar, device_id_type=MESH,
         )
 
-    def c_copy(i, slot, zz):
+    def c_copy(i, zi, zz):
         return pltpu.make_async_remote_copy(
-            src_ref=c_send.at[i], dst_ref=c_recv.at[slot], send_sem=c_ss.at[i],
-            recv_sem=c_rs.at[slot], device_id=rdev(zz, y, c), device_id_type=MESH,
-        )
+            src_ref=c_send.at[i, zi], dst_ref=c_recv.at[i // 4, z], send_sem=c_ss.at[i, zi],
+            recv_sem=c_rs.at[i // 4, z], device_id=rdev(zz, y, c), device_id_type=MESH,
+        )
+
+    def c_landed(hh, slot):
+        pltpu.make_async_remote_copy(
+            src_ref=c_send.at[0, 0], dst_ref=c_recv.at[hh, slot], send_sem=c_ss.at[0, 0],
+            recv_sem=c_rs.at[hh, slot], device_id=sib, device_id_type=MESH,
+        ).wait_recv()
 
     first_core = c == 0
     first_y = y == 0
 
     def compute(i):
-        k0 = pl.multiple_of(zoff(i) * CK, CK)
-        dk = dot(dsc[pl.ds(k0, CK), :], q[...], NN)
-        dv = dot(ex[pl.ds(k0, CK), :], do[...], NN)
-        for yy in range(2):
-            lo = slice(yy * 2 * PR, yy * 2 * PR + PR)
-            hi = slice(yy * 2 * PR + PR, yy * 2 * PR + 2 * PR)
-            for part_, g in ((0, dk), (1, dv)):
-                col = slice(part_ * HD, (part_ + 1) * HD)
-                a_keep[i, yy, :, col] = jnp.where(first_core, g[lo], g[hi])
-                a_send[i, yy, :, col] = jnp.where(first_core, g[hi], g[lo]).astype(BF)
+        def gather(ref):
+            picked = []
+            for zi in range(2):
+                k0 = zoff(2 * (i % 4) + zi) * CK + (i // 4) * HR
+                for b in range(4):
+                    picked.append(ref[pl.ds(pl.multiple_of(k0 + b * PR, HR), HR), :])
+            return jnp.concatenate(picked, axis=0)
+
+        for part_, g in ((0, dot(gather(dsc), q[...], NN)), (1, dot(gather(ex), do[...], NN))):
+            col = slice(part_ * HD, (part_ + 1) * HD)
+            for zi in range(2):
+                for yy in range(2):
+                    r0 = (zi * 4 + yy * 2) * HR
+                    lo, hi = g[r0 : r0 + HR], g[r0 + HR : r0 + 2 * HR]
+                    a_keep[i, zi, yy, :, col] = jnp.where(first_core, lo, hi)
+                    a_send[i, zi, yy, :, col] = jnp.where(first_core, hi, lo).astype(BF)
         a_copy(i).start()
 
     def after_a(i):
         a_copy(i).wait_recv()
-        s0 = a_keep[i, 0] + a_recv[i, 0].astype(F32)
-        s1 = a_keep[i, 1] + a_recv[i, 1].astype(F32)
+        s0 = a_keep[i, :, 0] + a_recv[i, :, 0].astype(F32)
+        s1 = a_keep[i, :, 1] + a_recv[i, :, 1].astype(F32)
         b_keep[i] = jnp.where(first_y, s0, s1)
         b_send[i] = jnp.where(first_y, s1, s0).astype(BF)
         b_copy(i).start()
 
-    def after_b(i):
+    def send_c(i):
         b_copy(i).wait_recv()
-        return b_keep[i] + b_recv[i].astype(F32)
-
-    def send_c(i):
-        c_send[i] = after_b(i).astype(BF)
-        c_copy(i, z, zoff(i)).start()
+        both = b_keep[i] + b_recv[i].astype(F32)
+        c_send[i] = both.astype(BF)
+        c_copy(i, 0, zoff(2 * (i % 4))).start()
+
+        @pl.when(i % 4 < 3)
+        def _():
+            c_copy(i, 1, zoff(2 * (i % 4) + 1)).start()
+
+        @pl.when(i % 4 == 3)
+        def _():
+            own_keep[i // 4] = both[1]
 
     def grads(i, carry):
         compute(i)
-
-        @pl.when(i >= 1)
-        def _():
-            after_a(i - 1)
-
-        @pl.when(i >= 2)
-        def _():
-            send_c(i - 2)
-
+        pl.when(i >= LAG_A)(lambda: after_a(i - LAG_A))
+        pl.when(i >= LAG_B)(lambda: send_c(i - LAG_B))
         return carry
 
     lax.fori_loop(0, 8, grads, 0)
-    after_a(7)
-    send_c(6)
+
+    def rest_a(i, carry):
+        after_a(i)
+        return carry
+
+    def rest_c(i, carry):
+        send_c(i)
+        return carry
+
+    lax.fori_loop(8 - LAG_A, 8, rest_a, 0)
+    lax.fori_loop(8 - LAG_B, 6, rest_c, 0)
     o_sdv[0] = dot(ex[own, 0:live_rows], do[0:live_rows, :], NN).astype(BF)
     o_sdk[0] = (dot(dsc[own, 0:live_rows], q[0:live_rows, :], NN) * SCALE).astype(BF)
-    summed = after_b(7)
-    for d in (1, 7, 2, 6, 3, 5, 4):
-        slot = (z + d) % 8
-        c_copy(0, slot, slot).wait_recv()
-        summed = summed + c_recv[slot].astype(F32)
-    dk = (summed[:, :HD] * SCALE).astype(BF)
-    dv = summed[:, HD:].astype(BF)
-    o_pdk[...] = dk
-    o_pdv[...] = dv
+    lax.fori_loop(6, 8, rest_c, 0)
+
+    copies[-2].wait()
+    copies[-1].wait()
+
+    def x_copy(send, recv, ss, rs, hh, k, side):
+        return pltpu.make_async_remote_copy(
+            src_ref=send.at[hh, k, side], dst_ref=recv.at[hh, k, side],
+            send_sem=ss.at[hh, k, side], recv_sem=rs.at[hh, k, side],
+            device_id=(xp, xm)[side], device_id_type=MESH,
+        )
+
+    def x1_copy(hh, k, side):
+        return x_copy(x1_send, x1_recv, x1_ss, x1_rs, hh, k, side)
+
+    def x2_copy(hh, k, side):
+        return x_copy(x2_send, x2_recv, x2_ss, x2_rs, hh, k, side)
+
+    def y_copy(hh, k):
+        return pltpu.make_async_remote_copy(
+            src_ref=y_send.at[hh, k], dst_ref=y_recv.at[k], send_sem=y_ss.at[k],
+            recv_sem=y_rs.at[k], device_id=hpar, device_id_type=MESH,
+        )
+
+    def piece(hh, k, xx, cols):
+        r0 = pl.multiple_of(xx * 8, 8)
+        return jnp.concatenate(
+            [part[hh, k, 0, pl.ds(r0, 8), cols], part[hh, k, 1, pl.ds(r0, 8), cols]], axis=0
+        )
+
+    halves = (slice(0, HW), slice(HW, CW))
+    ahead = ((x + 1) % 4, (x + 3) % 4)
+    far = (x + 2) % 4
+
+    def project(hh):
+        summed = own_keep[hh]
+        for d in (4, 3, 5, 2, 6, 1, 7):
+            slot = (z + d) % 8
+            c_landed(hh, slot)
+            summed = summed + c_recv[hh, slot].astype(F32)
+        dk = (summed[:, :HD] * SCALE).astype(BF)
+        dv = summed[:, HD:].astype(BF)
+        o_pdk[hh * HR : (hh + 1) * HR, :] = dk
+        o_pdv[hh * HR : (hh + 1) * HR, :] = dv
+        for k in range(NCOL):
+            for half in range(2):
+                rows = slice(half * (D // 2) + k * CW, half * (D // 2) + (k + 1) * CW)
+                part[hh, k, half] = dot(dk, kw[rows, :], NT) + dot(dv, vw[rows, :], NT)
+            for side in range(2):
+                x1_send[hh, k, side, 0] = piece(hh, k, far, halves[side]).astype(BF)
+                x1_send[hh, k, side, 1] = piece(hh, k, ahead[side], halves[1 - side]).astype(BF)
+                x1_copy(hh, k, side).start()
+
+    def second(hh):
+        for k in range(NCOL):
+            for side in range(2):
+                x1_copy(hh, k, side).wait_recv()
+                mine = piece(hh, k, ahead[side], halves[side])
+                x2_send[hh, k, side] = (mine + x1_recv[hh, k, side, 0].astype(F32)).astype(BF)
+                x2_copy(hh, k, side).start()
+
+    def third(hh):
+        for k in range(NCOL):
+            for side in range(2):
+                x2_copy(hh, k, side).wait_recv()
+            for half in range(2):
+                got = (
+                    piece(hh, k, x, halves[half])
+                    + x2_recv[hh, k, half].astype(F32)
+                    + x1_recv[hh, k, 1 - half, 1].astype(F32)
+                )
+                y_keep[hh, k, :, halves[half]] = got
+                y_send[hh, k, :, halves[half]] = got.astype(BF)
+            pl.when(yh != hh)(lambda: y_copy(hh, k).start())
+
+    project(0)
+    project(1)
+    second(0)
+    second(1)
+    third(0)
+    third(1)
+    for k in range(NCOL):
+        y_copy(0, k).wait_recv()
+        full = y_keep[yh, k] + y_recv[k].astype(F32)
+        o_in[:, k * CW : (k + 1) * CW] = full[0:8].astype(BF)
+        o_in[:, D // 2 + k * CW : D // 2 + (k + 1) * CW] = full[8:16].astype(BF)
     for i in range(8):
         a_copy(i).wait_send()
         b_copy(i).wait_send()
-    for i in range(7):
-        c_copy(i, z, zoff(i)).wait_send()
-    copies[-2].wait()
-    copies[-1].wait()
-
-    def x_copy(send, recv, ss, rs, k, side):
-        return pltpu.make_async_remote_copy(
-            src_ref=send.at[k, side], dst_ref=recv.at[k, side], send_sem=ss.at[k, side],
-            recv_sem=rs.at[k, side], device_id=(xp, xm)[side], device_id_type=MESH,
-        )
-
-    def y_copy(k):
-        return pltpu.make_async_remote_copy(
-            src_ref=y_send.at[k], dst_ref=y_recv.at[k], send_sem=y_ss.at[k],
-            recv_sem=y_rs.at[k], device_id=hpar, device_id_type=MESH,
-        )
-
-    def piece(k, hh, xx, cols):
-        r0 = pl.multiple_of((hh * 4 + xx) * 8, 8)
-        return jnp.concatenate(
-            [part[k, 0, pl.ds(r0, 8), cols], part[k, 1, pl.ds(r0, 8), cols]], axis=0
-        )
-
-    halves = (slice(0, HW), slice(HW, CW))
-    ahead = ((x + 1) % 4, (x + 3) % 4)
-    far = (x + 2) % 4
-
+        c_copy(i, 0, z).wait_send()
+        if i % 4 < 3:
+            c_copy(i, 1, z).wait_send()
     for k in range(NCOL):
-        for half in range(2):
-            rows = slice(half * (D // 2) + k * CW, half * (D // 2) + (k + 1) * CW)
-            part[k, half] = dot(dk, kw[rows, :], NT) + dot(dv, vw[rows, :], NT)
-        for side in range(2):
-            for hh in range(2):
-                x1_send[k, side, 0, hh] = piece(k, hh, far, halves[side]).astype(BF)
-                x1_send[k, side, 1, hh] = piece(k, hh, ahead[side], halves[1 - side]).astype(BF)
-            x_copy(x1_send, x1_recv, x1_ss, x1_rs, k, side).start()
-    for k in range(NCOL):
-        for side in range(2):
-            x_copy(x1_send, x1_recv, x1_ss, x1_rs, k, side).wait_recv()
-            for hh in range(2):
-                mine = piece(k, hh, ahead[side], halves[side])
-                x2_send[k, side, hh] = (mine + x1_recv[k, side, 0, hh].astype(F32)).astype(BF)
-            x_copy(x2_send, x2_recv, x2_ss, x2_rs, k, side).start()
-    for k in range(NCOL):
-        for side in range(2):
-            x_copy(x2_send, x2_recv, x2_ss, x2_rs, k, side).wait_recv()
-        for half in range(2):
-            def gathered(hh):
-                return (
-                    piece(k, hh, x, halves[half])
-                    + x2_recv[k, half, hh].astype(F32)
-                    + x1_recv[k, 1 - half, 1, hh].astype(F32)
-                )
-
-            y_keep[k, :, halves[half]] = gathered(yh)
-            y_send[k, :, halves[half]] = gathered(1 - yh).astype(BF)
-        y_copy(k).start()
-    for k in range(NCOL):
-        y_copy(k).wait_recv()
-        full = y_keep[k] + y_recv[k].astype(F32)
-        o_in[:, k * CW : (k + 1) * CW] = full[0:8].astype(BF)
-        o_in[:, D // 2 + k * CW : D // 2 + (k + 1) * CW] = full[8:16].astype(BF)
-    for k in range(NCOL):
-        for side in range(2):
-            x_copy(x1_send, x1_recv, x1_ss, x1_rs, k, side).wait_send()
-            x_copy(x2_send, x2_recv, x2_ss, x2_rs, k, side).wait_send()
-        y_copy(k).wait_send()
+        for hh in range(2):
+            for side in range(2):
+                x1_copy(hh, k, side).wait_send()
+                x2_copy(hh, k, side).wait_send()
+        y_copy(0, k).wait_send()
 
 
 def hand_on_kernel(*refs):
@@ -427,21 +469,22 @@
             pltpu.VMEM((2, KEYS + SR, SR), F32),
             pltpu.VMEM((D, HD), BF),
             pltpu.VMEM((D, HD), BF),
-            pltpu.VMEM((8, 2, PR, 2 * HD), BF),
-            pltpu.VMEM((8, 2, PR, 2 * HD), F32),
-            pltpu.VMEM((8, 2, PR, 2 * HD), BF),
-            pltpu.VMEM((8, PR, 2 * HD), BF),
-            pltpu.VMEM((8, PR, 2 * HD), F32),
-            pltpu.VMEM((8, PR, 2 * HD), BF),
-            pltpu.VMEM((8, PR, 2 * HD), BF),
-            pltpu.VMEM((8, PR, 2 * HD), BF),
-            pltpu.VMEM((NCOL, 2, 64, CW), F32),
-            pltpu.VMEM((NCOL, 2, 2, 2, 16, HW), BF),
-            pltpu.VMEM((NCOL, 2, 2, 2, 16, HW), BF),
-            pltpu.VMEM((NCOL, 2, 2, 16, HW), BF),
-            pltpu.VMEM((NCOL, 2, 2, 16, HW), BF),
-            pltpu.VMEM((NCOL, 16, CW), F32),
-            pltpu.VMEM((NCOL, 16, CW), BF),
+            pltpu.VMEM((8, 2, 2, HR, 2 * HD), BF),
+            pltpu.VMEM((8, 2, 2, HR, 2 * HD), F32),
+            pltpu.VMEM((8, 2, 2, HR, 2 * HD), BF),
+            pltpu.VMEM((8, 2, HR, 2 * HD), BF),
+            pltpu.VMEM((8, 2, HR, 2 * HD), F32),
+            pltpu.VMEM((8, 2, HR, 2 * HD), BF),
+            pltpu.VMEM((8, 2, HR, 2 * HD), BF),
+            pltpu.VMEM((2, 8, HR, 2 * HD), BF),
+            pltpu.VMEM((2, HR, 2 * HD), F32),
+            pltpu.VMEM((2, NCOL, 2, HR, CW), F32),
+            pltpu.VMEM((2, NCOL, 2, 2, 16, HW), BF),
+            pltpu.VMEM((2, NCOL, 2, 2, 16, HW), BF),
+            pltpu.VMEM((2, NCOL, 2, 16, HW), BF),
+            pltpu.VMEM((2, NCOL, 2, 16, HW), BF),
+            pltpu.VMEM((2, NCOL, 16, CW), F32),
+            pltpu.VMEM((2, NCOL, 16, CW), BF),
             pltpu.VMEM((NCOL, 16, CW), BF),
             dma((44,)),
             dma((31,)),
@@ -450,12 +493,12 @@
             dma((8,)),
             dma((8,)),
             dma((8,)),
-            dma((8,)),
-            dma((8,)),
-            dma((NCOL, 2)),
-            dma((NCOL, 2)),
-            dma((NCOL, 2)),
-            dma((NCOL, 2)),
+            dma((8, 2)),
+            dma((2, 8)),
+            dma((2, NCOL, 2)),
+            dma((2, NCOL, 2)),
+            dma((2, NCOL, 2)),
+            dma((2, NCOL, 2)),
             dma((NCOL,)),
             dma((NCOL,)),
         ],

time: 76.7 us -> 72 us (0.939)
  Pallas kernels: 75 us -> 70.6 us
    pallas_call x1, Pallas kernels: 72.9 us -> 68.4 us  [body(): pl.pallas_call(body_kernel, in_specs=[anyspec] * 8 + [sspec] + [anyspec]...]
where the time goes in v3:
time: 72 us; the launch traced here: 71.9 us
  Pallas kernels  70.6 us (98%)
  between operations  1.29 us (2%)
    pallas_call x1, Pallas kernels, body(): pl.pallas_call(body_kernel, in_specs=[anyspec] * 8 + [sspec] + [anyspec]...  68.4 us
    pallas_call x1, Pallas kernels, hand_on(): pl.pallas_call(hand_on_kernel, in_specs=[vspec] * len(arrays), out_specs=...  2.16 us

profile of v3, /device:TPU:32, one launch (start us, length us, event | category | flops | bytes accessed | tf_op | source)
XLA Modules:
  0.0 71.9 jit_solution(4790097285154073313)
XLA Ops:
  1.3 68.4 %shard_map.162 = (bf16[64,1024]{1,0:T(8,128)(2,1)}, bf16[64,128]{1,0:T(8,128)(2,1)}, bf16[64,128]{1,0:T(8,128)(2,1)}, bf16[1,256,1024]{2,1,0:T(8,128)(2,1)}, bf1...) custom-call(bf16[64,1024]{1,0:T(8,128)(2,1)} %pq.1, bf16[64,128]{1,0:T(8,128)(2,1)} %pk.1, ...), custom_call_target="tpu_custom_call" | custom-call | tf_op jit(solution)/shard_map/pallas_call | solution.py:448
  69.7 2.2 %shard_map.163 = (bf16[64,1024]{1,0:T(8,128)(2,1)}, bf16[64,128]{1,0:T(8,128)(2,1)}, bf16[64,128]{1,0:T(8,128)(2,1)}, bf16[1,256,1024]{2,1,0:T(8,128)(2,1)}, bf1...) custom-call(bf16[64,1024]{1,0:T(8,128)(2,1)} %get-tuple-element.14.refs_0_, ...), custom_call_target="tpu_custom_call" | custom-call | tf_op jit(solution)/shard_map/pallas_call | solution.py:432

commit v4 on v3

--- a/solution.py
+++ b/solution.py
@@ -42,7 +42,7 @@
 def body_kernel(
     pq, pk, pv, pdo, sq, sk, sv, sdo, ln, kw_hbm, vw_hbm,
     o_pdq, o_pdk, o_pdv, o_sdq, o_sdk, o_sdv, o_in,
-    kv, kt, q, do, ex, dsc, dp_s, s_s, kw, vw,
+    kv, kt, q, do, ex, dsc, dp_s, s_s, kvw,
     a_send, a_keep, a_recv, b_send, b_keep, b_recv, c_send, c_recv, own_keep,
     part, x1_send, x1_recv, x2_send, x2_recv, y_keep, y_send, y_recv,
     loc, ag_s, ag_r, a_ss, a_rs, b_ss, b_rs, c_ss, c_rs,
@@ -87,8 +87,8 @@
     for i in range(4):
         local(sk.at[0, i * PR : (i + 1) * PR, :], kv.at[ROLL + i, 0])
         local(sv.at[0, i * PR : (i + 1) * PR, :], kv.at[ROLL + i, 1])
-    local(kw_hbm, kw)
-    local(vw_hbm, vw)
+    local(kw_hbm, kvw.at[:, 0:HD])
+    local(vw_hbm, kvw.at[:, HD : 2 * HD])
 
     barrier = pltpu.get_barrier_semaphore()
     peers = [rdev((z + d) % 8, y, c) for d in range(1, 8)] + [sib, ypar, xp, xm, hpar]
@@ -142,8 +142,6 @@
         return kv[4 * i : 4 * i + 4, 1].reshape(CK, HD)
 
     n_live = ln[0]
-    for i in range(9):
-        kt[:, i * CK : (i + 1) * CK] = keys(i).T
     live = lax.broadcasted_iota(jnp.int32, (SR, HD), 0) < n_live
     for h in range(HEADS):
         rows = slice(h * SR, (h + 1) * SR)
@@ -159,7 +157,7 @@
     def causal_mask(i, s):
         return jnp.where(kpos + i * CK <= roll * PR + (qpos & (PR - 1)), s, NEG)
 
-    def tile(t, slot, chunks, mask, finish):
+    def tile(t, slot, chunks, mask):
         r0 = pl.multiple_of(t * SR, SR)
         cols = pl.ds(r0, SR)
         qt = q[cols, :]
@@ -184,42 +182,51 @@
         inv = 1.0 / jnp.sum(total, axis=0, keepdims=True)
         delta = jnp.sum(delta, axis=0, keepdims=True) * inv
         yield
-        acc = jnp.zeros((HD, SR), F32)
         for i in range(chunks):
             rows = slice(i * CK, (i + 1) * CK)
             p = s_s[slot, rows, :] * inv
             ds = (p * (dp_s[slot, rows, :] - delta)).astype(BF)
             ex[rows, cols] = p.astype(BF)
             dsc[rows, cols] = ds
-            acc = acc + dot(kt[:, rows], ds, NN)
-        finish(t, (acc * SCALE).T.astype(BF))
         yield
 
-    def pair(t, chunks, mask, finish):
-        tiles = [tile(2 * t + slot, slot, chunks, mask, finish) for slot in range(2)]
+    def pair(t, chunks, mask):
+        tiles = [tile(2 * t + slot, slot, chunks, mask) for slot in range(2)]
         for _ in range(3):
             for one in tiles:
                 next(one)
 
-    def roll_out(t, dq):
-        o_sdq[0, :, pl.ds(pl.multiple_of(t * HD, HD), HD)] = dq
-
     def roll_pair(t, carry):
-        pair(t, 9, own_mask, roll_out)
+        pair(t, 9, own_mask)
         return carry
 
     lax.fori_loop(0, HEADS // 2, roll_pair, 0)
 
-    def prompt_out(t, dq):
+    def prompt_pair(t, carry):
+        pair(t, 8, causal_mask)
+        return carry
+
+    lax.fori_loop(HEADS // 2, HEADS // 2 + 1, prompt_pair, 0)
+
+    def turn_keys():
+        for i in range(9):
+            kt[:, i * CK : (i + 1) * CK] = keys(i).T
+
+    def query_grad(t, rows):
+        cols = pl.ds(pl.multiple_of(t * SR, SR), SR)
+        return (dot(kt[:, 0:rows], dsc[0:rows, cols], NN) * SCALE).T.astype(BF)
+
+    def roll_query(t, carry):
+        o_sdq[0, :, pl.ds(pl.multiple_of(t * HD, HD), HD)] = query_grad(t, KEYS + SR)
+        return carry
+
+    def roll_queries(first, last):
+        lax.fori_loop(first, last, roll_query, 0)
+
+    def prompt_query(i):
+        dq = query_grad(HEADS + i, KEYS)
         for h in range(4):
-            col = pl.multiple_of(((t - HEADS) * 4 + h) * HD, HD)
-            o_pdq[:, pl.ds(col, HD)] = dq[h * PR : (h + 1) * PR, :]
-
-    def prompt_pair(t, carry):
-        pair(t, 8, causal_mask, prompt_out)
-        return carry
-
-    lax.fori_loop(HEADS // 2, HEADS // 2 + 1, prompt_pair, 0)
+            o_pdq[:, (4 * i + h) * HD : (4 * i + h + 1) * HD] = dq[h * PR : (h + 1) * PR, :]
 
     own = slice(KEYS, KEYS + SR)
     live_rows = HEADS * SR
@@ -313,6 +320,7 @@
 
     lax.fori_loop(8 - LAG_A, 8, rest_a, 0)
     lax.fori_loop(8 - LAG_B, 6, rest_c, 0)
+    turn_keys()
     o_sdv[0] = dot(ex[own, 0:live_rows], do[0:live_rows, :], NN).astype(BF)
     o_sdk[0] = (dot(dsc[own, 0:live_rows], q[0:live_rows, :], NN) * SCALE).astype(BF)
     lax.fori_loop(6, 8, rest_c, 0)
@@ -359,10 +367,11 @@
         dv = summed[:, HD:].astype(BF)
         o_pdk[hh * HR : (hh + 1) * HR, :] = dk
         o_pdv[hh * HR : (hh + 1) * HR, :] = dv
+        both = jnp.concatenate([dk, dv], axis=1)
         for k in range(NCOL):
             for half in range(2):
                 rows = slice(half * (D // 2) + k * CW, half * (D // 2) + (k + 1) * CW)
-                part[hh, k, half] = dot(dk, kw[rows, :], NT) + dot(dv, vw[rows, :], NT)
+                part[hh, k, half] = dot(both, kvw[rows, :], NT)
             for side in range(2):
                 x1_send[hh, k, side, 0] = piece(hh, k, far, halves[side]).astype(BF)
                 x1_send[hh, k, side, 1] = piece(hh, k, ahead[side], halves[1 - side]).astype(BF)
@@ -391,11 +400,17 @@
             pl.when(yh != hh)(lambda: y_copy(hh, k).start())
 
     project(0)
+    roll_queries(0, 2)
     project(1)
     second(0)
+    roll_queries(2, 5)
     second(1)
     third(0)
+    roll_queries(5, 7)
     third(1)
+    roll_queries(7, 8)
+    prompt_query(0)
+    prompt_query(1)
     for k in range(NCOL):
         y_copy(0, k).wait_recv()
         full = y_keep[yh, k] + y_recv[k].astype(F32)
@@ -416,25 +431,29 @@
 
 
 def hand_on_kernel(*refs):
-    count = len(refs) // 2
-    copies = []
-    for i in range(count):
-        cp = pltpu.make_async_copy(refs[i], refs[count + i], refs[-1].at[i])
+    count = (len(refs) - 2) // 3
+    stage, arrive, leave = refs[2 * count : 3 * count], refs[-2], refs[-1]
+    loads = [pltpu.make_async_copy(refs[i], stage[i], arrive.at[i]) for i in range(count)]
+    stores = [pltpu.make_async_copy(stage[i], refs[count + i], leave.at[i]) for i in range(count)]
+    for cp in loads:
         cp.start()
-        copies.append(cp)
-    for cp in copies:
+    for load, store in zip(loads, stores):
+        load.wait()
+        store.start()
+    for cp in stores:
         cp.wait()
 
 
 def hand_on(arrays):
     spec = pl.BlockSpec(memory_space=pl.ANY)
-    vspec = pl.BlockSpec(memory_space=pltpu.VMEM)
+    count = len(arrays)
     return pl.pallas_call(
         hand_on_kernel,
-        in_specs=[vspec] * len(arrays),
-        out_specs=[spec] * len(arrays),
+        in_specs=[spec] * count,
+        out_specs=[spec] * count,
         out_shape=[jax.ShapeDtypeStruct(a.shape, a.dtype) for a in arrays],
-        scratch_shapes=[pltpu.SemaphoreType.DMA((len(arrays),))],
+        scratch_shapes=[pltpu.VMEM(a.shape, a.dtype) for a in arrays]
+        + [pltpu.SemaphoreType.DMA((count,))] * 2,
     )(*arrays)
 
 
@@ -467,8 +486,7 @@
             pltpu.VMEM((KEYS + SR, rows), BF),
             pltpu.VMEM((2, KEYS + SR, SR), F32),
             pltpu.VMEM((2, KEYS + SR, SR), F32),
-            pltpu.VMEM((D, HD), BF),
-            pltpu.VMEM((D, HD), BF),
+            pltpu.VMEM((D, 2 * HD), BF),
             pltpu.VMEM((8, 2, 2, HR, 2 * HD), BF),
             pltpu.VMEM((8, 2, 2, HR, 2 * HD), F32),
             pltpu.VMEM((8, 2, 2, HR, 2 * HD), BF),

time: 72 us -> 70.3 us (0.976)
  Pallas kernels: 70.6 us -> 68.9 us
    pallas_call x1, Pallas kernels: 68.4 us -> 66.8 us  [body(): pl.pallas_call(body_kernel, in_specs=[anyspec] * 8 + [sspec] + [anyspec]...]
where the time goes in v4:
time: 70.3 us; the launch traced here: 70.2 us
  Pallas kernels  68.9 us (98%)
  between operations  1.29 us (2%)
    pallas_call x1, Pallas kernels, body(): pl.pallas_call(body_kernel, in_specs=[anyspec] * 8 + [sspec] + [anyspec]...  66.8 us
    pallas_call x1, Pallas kernels, hand_on(): pl.pallas_call(hand_on_kernel, in_specs=[spec] * count, out_specs=[spec]...  2.15 us

profile of v4, /device:TPU:32, one launch (start us, length us, event | category | flops | bytes accessed | tf_op | source)
XLA Modules:
  0.0 70.2 jit_solution(9315168862763030354)
XLA Ops:
  1.3 66.8 %shard_map.162 = (bf16[64,1024]{1,0:T(8,128)(2,1)}, bf16[64,128]{1,0:T(8,128)(2,1)}, bf16[64,128]{1,0:T(8,128)(2,1)}, bf16[1,256,1024]{2,1,0:T(8,128)(2,1)}, bf1...) custom-call(bf16[64,1024]{1,0:T(8,128)(2,1)} %pq.1, bf16[64,128]{1,0:T(8,128)(2,1)} %pk.1, ...), custom_call_target="tpu_custom_call" | custom-call | tf_op jit(solution)/shard_map/pallas_call | solution.py:467
  68.1 2.1 %shard_map.163 = (bf16[64,1024]{1,0:T(8,128)(2,1)}, bf16[64,128]{1,0:T(8,128)(2,1)}, bf16[64,128]{1,0:T(8,128)(2,1)}, bf16[1,256,1024]{2,1,0:T(8,128)(2,1)}, bf1...) custom-call(bf16[64,1024]{1,0:T(8,128)(2,1)} %get-tuple-element.14.refs_0_, ...), custom_call_target="tpu_custom_call" | custom-call | tf_op jit(solution)/shard_map/pallas_call | solution.py:450

commit v5 on v4

--- a/solution.py
+++ b/solution.py
@@ -24,7 +24,7 @@
 NN = (((1,), (0,)), ((), ()))
 MESH = pl.DeviceIdType.MESH
 D = 8192
-NCOL = 4
+NCOL = 2
 CW = D // 2 // NCOL
 HW = CW // 2
 LAG_A = 2

time: 70.3 us -> 70.3 us (level)
  no operation moved by 1% of the time
where the time goes in v5:
time: 70.3 us; the launch traced here: 70.2 us
  Pallas kernels  68.9 us (98%)
  between operations  1.29 us (2%)
    pallas_call x1, Pallas kernels, body(): pl.pallas_call(body_kernel, in_specs=[anyspec] * 8 + [sspec] + [anyspec]...  66.8 us
    pallas_call x1, Pallas kernels, hand_on(): pl.pallas_call(hand_on_kernel, in_specs=[spec] * count, out_specs=[spec]...  2.15 us

profile of v5, /device:TPU:32, one launch (start us, length us, event | category | flops | bytes accessed | tf_op | source)
XLA Modules:
  0.0 70.2 jit_solution(10687886827624091085)
XLA Ops:
  1.3 66.8 %shard_map.162 = (bf16[64,1024]{1,0:T(8,128)(2,1)}, bf16[64,128]{1,0:T(8,128)(2,1)}, bf16[64,128]{1,0:T(8,128)(2,1)}, bf16[1,256,1024]{2,1,0:T(8,128)(2,1)}, bf1...) custom-call(bf16[64,1024]{1,0:T(8,128)(2,1)} %pq.1, bf16[64,128]{1,0:T(8,128)(2,1)} %pk.1, ...), custom_call_target="tpu_custom_call" | custom-call | tf_op jit(solution)/shard_map/pallas_call | solution.py:467
  68.0 2.1 %shard_map.163 = (bf16[64,1024]{1,0:T(8,128)(2,1)}, bf16[64,128]{1,0:T(8,128)(2,1)}, bf16[64,128]{1,0:T(8,128)(2,1)}, bf16[1,256,1024]{2,1,0:T(8,128)(2,1)}, bf1...) custom-call(bf16[64,1024]{1,0:T(8,128)(2,1)} %get-tuple-element.14.refs_0_, ...), custom_call_target="tpu_custom_call" | custom-call | tf_op jit(solution)/shard_map/pallas_call | solution.py:450
